TPU v7x, 256 devices: a whole 4x4x8 slice. The times are simulated.
256 devices in a mesh: replica: 16 (over y_lo, z), section: 4 (over y_hi, core), shard: 4 (over x).
Axes of the slice: x: 4, y: 4 (y_hi: 2, y_lo: 2; y = y_hi * 2 + y_lo), z: 8, core: 2. Of those that a mesh axis runs over, the one named last changes fastest.
Arguments:
- inputs: bfloat16 [16, 1, 128, 1024], P('replica', None, None, 'shard'), may hold values from -17 to 17
- targets: bfloat16 [16, 1, 128, 1024], P('replica', None, None, 'shard'), may hold values from -6 to 6
- weight_a: bfloat16 [16, 4, 1024, 3072], P('replica', 'section', None, 'shard'), may hold values from -6 to 6
- weight_b: bfloat16 [16, 4, 3072, 1024], P('replica', 'section', 'shard'), may hold values from -6 to 6
- moment_a: bfloat16 [16, 4, 1024, 3072], P('replica', 'section', None, 'shard'), may hold values from -3 to 3
- moment_b: bfloat16 [16, 4, 3072, 1024], P('replica', 'section', 'shard'), may hold values from -3 to 3
- routes: int32 [1, 3, 16, 16], replicated, may hold values from 0 to 15, each once within a row
- partners: int32 [4, 2, 16, 16], replicated, may hold values from 0 to 15, as said below
Outputs:
- new_weight_a: bfloat16 [16, 4, 1024, 3072], P('replica', 'section', None, 'shard')
- new_weight_b: bfloat16 [16, 4, 3072, 1024], P('replica', 'section', 'shard')
- new_moment_a: bfloat16 [16, 4, 1024, 3072], P('replica', 'section', None, 'shard')
- new_moment_b: bfloat16 [16, 4, 3072, 1024], P('replica', 'section', 'shard')
Inputs may be any that keep to these rules, and one draw needn't show every extreme that they name: Each routes[m, s, q, :] names every replica once, so each replica of section s + 1 receives exactly one block from every replica of section s. For each section s, projection t and piece k, partners[s, t, k, :] is its own inverse (the partner of the partner is the replica itself); for each s, t and replica r, partners[s, t, :, r] names every replica once, and exactly one piece pairs r with itself.
All inputs are finite; a program needn't handle non-finite values.
Results may differ from a plain program's by a relative error of at most 0.022.
Values may be sent and summed in bfloat16 or wider, within the bound.
A program may use at most 128 MiB of HBM per device.

v0:
```python
import math

import jax
import jax.numpy as jnp
from jax import lax
from jax.sharding import PartitionSpec as P

epsilon = 1e-05
inner_rate = 0.5
momentum_decay = 0.9
outer_rate = 0.7


def shifted(array, axis, by):
    size = lax.axis_size(axis)
    pairs = [(i, i + by) for i in range(size) if 0 <= i + by < size]
    return lax.ppermute(array, axis, pairs)


def norm_scale(gathered):
    wide = gathered.astype(jnp.float32)
    return lax.rsqrt(jnp.mean(wide * wide, axis=1, keepdims=True) + epsilon)


def keep_slot(store, value, place, valid):
    old_value = lax.dynamic_index_in_dim(store, place, 0, keepdims=False)
    return lax.dynamic_update_index_in_dim(store, jnp.where(valid, value, old_value), place, 0)


def pair_mix(weights, moments, deltas, far_weights, far_moments, far_deltas):
    mean_weight = (weights.astype(jnp.float32) + far_weights.astype(jnp.float32)) * 0.5
    mean_moment = (moments.astype(jnp.float32) + far_moments.astype(jnp.float32)) * 0.5
    mean_delta = (deltas.astype(jnp.float32) + far_deltas.astype(jnp.float32)) * 0.5
    new_moment = momentum_decay * mean_moment + mean_delta
    new_weight = mean_weight - outer_rate * (momentum_decay * new_moment + mean_delta)
    return (new_weight.astype(jnp.bfloat16), new_moment.astype(jnp.bfloat16))


def per_device(inputs, targets, weight_a, weight_b, moment_a, moment_b, routes, partners):
    replicas = lax.axis_size("replica")
    sections = lax.axis_size("section")
    replica_id = lax.axis_index("replica")
    section_id = lax.axis_index("section")
    shard_id = lax.axis_index("shard")
    batches = inputs.shape[1]
    row_count = inputs.shape[2]
    features = inputs.shape[3]
    width = weight_a.shape[2]
    local_hidden = weight_a.shape[3]
    hidden_total = local_hidden * lax.axis_size("shard")
    scale_in = 1.0 / math.sqrt(width)
    scale_out = 1.0 / math.sqrt(hidden_total)
    weight_in = weight_a[0, 0]
    weight_out = weight_b[0, 0]
    ticks = batches + sections - 1
    group_rows = row_count // replicas
    labels = jnp.arange(replicas, dtype=jnp.int32)

    def table_row(batch_index, link):
        batch_clip = jnp.clip(batch_index, 0, batches - 1)
        link_clip = jnp.clip(link, 0, sections - 2)
        return routes[batch_clip, link_clip, replica_id]

    def by_target(destination):
        match = (destination[None, :] == labels[:, None]).astype(jnp.int32)
        return jnp.sum(labels[None, :] * match, axis=1)

    incoming = jnp.zeros((row_count, features), jnp.bfloat16)
    kept_inputs = jnp.zeros((batches, row_count, width), jnp.bfloat16)
    kept_preact = jnp.zeros((batches, row_count, local_hidden), jnp.float32)
    kept_output = jnp.zeros((batches, row_count, features), jnp.bfloat16)
    for tick_index in range(ticks):
        batch_index = tick_index - section_id
        valid = (batch_index >= 0) & (batch_index < batches)
        place = jnp.clip(batch_index, 0, batches - 1)
        own_rows = lax.dynamic_index_in_dim(inputs[0], place, 0, keepdims=False)
        current = jnp.where(section_id == 0, own_rows, incoming)
        gathered = lax.all_gather(current, "shard", axis=1, tiled=True)
        inverse_rms = norm_scale(gathered)
        normed = (gathered.astype(jnp.float32) * inverse_rms).astype(jnp.bfloat16)
        preact = jnp.dot(normed, weight_in, preferred_element_type=jnp.float32) * scale_in
        hidden = jax.nn.silu(preact).astype(jnp.bfloat16)
        term = jnp.dot(hidden, weight_out, preferred_element_type=jnp.float32) * scale_out
        total = lax.psum_scatter(
            term.astype(jnp.bfloat16), "shard", scatter_dimension=1, tiled=True
        ).astype(jnp.float32)
        output = (current.astype(jnp.float32) + total).astype(jnp.bfloat16)
        kept_inputs = keep_slot(kept_inputs, gathered, place, valid)
        kept_preact = keep_slot(kept_preact, preact, place, valid)
        kept_output = keep_slot(kept_output, output, place, valid)
        if tick_index + 1 < ticks:
            order = by_target(table_row(tick_index - section_id, section_id))
            send_grouped = jnp.take(output.reshape(replicas, group_rows, features), order, axis=0)
            send_mixed = lax.all_to_all(
                send_grouped, "replica", split_axis=0, concat_axis=0, tiled=True
            )
            incoming = shifted(send_mixed.reshape(row_count, features), "section", 1)
    section_tables = lax.dynamic_index_in_dim(partners, section_id, 0, keepdims=False)
    destination_in = section_tables[0][:, replica_id]
    destination_out = section_tables[1][:, replica_id]
    order_in = by_target(destination_in)
    order_out = by_target(destination_out)

    def arrange_in(array):
        return jnp.take(array.reshape(replicas, width // replicas, local_hidden), order_in, axis=0)

    def arrange_out(array):
        return jnp.take(array.reshape(replicas, local_hidden // replicas, width), order_out, axis=0)

    state_in = arrange_in(weight_in)
    moment_in = arrange_in(moment_a[0, 0])
    state_out = arrange_out(weight_out)
    moment_out = arrange_out(moment_b[0, 0])
    incoming = jnp.zeros((row_count, features), jnp.bfloat16)
    grad_in = jnp.zeros((width, local_hidden), jnp.float32)
    grad_out = jnp.zeros((local_hidden, width), jnp.float32)
    contract_rows = (((0,), (0,)), ((), ()))
    contract_last = (((1,), (1,)), ((), ()))
    for tick_index in range(ticks):
        batch_index = tick_index - (sections - 1 - section_id)
        valid = (batch_index >= 0) & (batch_index < batches)
        place = jnp.clip(batch_index, 0, batches - 1)
        last_output = lax.dynamic_index_in_dim(kept_output, place, 0, keepdims=False)
        goal_rows = lax.dynamic_index_in_dim(targets[0], place, 0, keepdims=False)
        own_grad = (last_output.astype(jnp.float32) - goal_rows.astype(jnp.float32)).astype(
            jnp.bfloat16
        )
        upstream = jnp.where(section_id == sections - 1, own_grad, incoming)
        upstream = jnp.where(valid, upstream, jnp.zeros_like(upstream))
        gathered_up = lax.all_gather(upstream, "shard", axis=1, tiled=True)
        gathered = lax.dynamic_index_in_dim(kept_inputs, place, 0, keepdims=False)
        preact = lax.dynamic_index_in_dim(kept_preact, place, 0, keepdims=False)
        inverse_rms = norm_scale(gathered)
        normed = (gathered.astype(jnp.float32) * inverse_rms).astype(jnp.bfloat16)
        hidden = jax.nn.silu(preact).astype(jnp.bfloat16)
        grad_out = (
            grad_out
            + lax.dot_general(
                hidden, gathered_up, contract_rows, preferred_element_type=jnp.float32
            )
            * scale_out
        )
        grad_hidden = (
            lax.dot_general(
                gathered_up, weight_out, contract_last, preferred_element_type=jnp.float32
            )
            * scale_out
        )
        gate = jax.nn.sigmoid(preact)
        grad_pre = (grad_hidden * gate * (1.0 + preact * (1.0 - gate))).astype(jnp.bfloat16)
        grad_in = (
            grad_in
            + lax.dot_general(normed, grad_pre, contract_rows, preferred_element_type=jnp.float32)
            * scale_in
        )
        term = (
            lax.dot_general(grad_pre, weight_in, contract_last, preferred_element_type=jnp.float32)
            * scale_in
        )
        total = lax.psum_scatter(
            term.astype(jnp.bfloat16), "shard", scatter_dimension=1, tiled=True
        ).astype(jnp.float32)
        exact = (
            lax.dynamic_slice_in_dim(gathered, shard_id * features, features, 1).astype(jnp.float32)
            * inverse_rms
        )
        along = lax.psum(jnp.sum(total * exact, axis=1), "shard") / width
        result = (
            upstream.astype(jnp.float32) + inverse_rms * (total - exact * along[:, None])
        ).astype(jnp.bfloat16)
        if tick_index + 1 < ticks:
            send_destination = table_row(tick_index - sections + 2 + section_id, section_id)
            grouped = result.reshape(replicas, group_rows, features)
            mixed = lax.all_to_all(grouped, "replica", split_axis=0, concat_axis=0, tiled=True)
            moved = shifted(mixed, "section", -1)
            incoming = jnp.take(moved, send_destination, axis=0).reshape(row_count, features)
    delta_in = arrange_in((inner_rate * grad_in).astype(jnp.bfloat16))
    delta_out = arrange_out((inner_rate * grad_out).astype(jnp.bfloat16))
    far_state_in, far_moment_in, far_delta_in, far_state_out, far_moment_out, far_delta_out = (
        lax.all_to_all(state_in, "replica", split_axis=0, concat_axis=0, tiled=True),
        lax.all_to_all(moment_in, "replica", split_axis=0, concat_axis=0, tiled=True),
        lax.all_to_all(delta_in, "replica", split_axis=0, concat_axis=0, tiled=True),
        lax.all_to_all(state_out, "replica", split_axis=0, concat_axis=0, tiled=True),
        lax.all_to_all(moment_out, "replica", split_axis=0, concat_axis=0, tiled=True),
        lax.all_to_all(delta_out, "replica", split_axis=0, concat_axis=0, tiled=True),
    )
    new_in, new_moment_in = pair_mix(
        state_in, moment_in, delta_in, far_state_in, far_moment_in, far_delta_in
    )
    new_out, new_moment_out = pair_mix(
        state_out, moment_out, delta_out, far_state_out, far_moment_out, far_delta_out
    )
    shape_in = (1, 1, width, local_hidden)
    shape_out = (1, 1, local_hidden, width)
    new_weight_a = jnp.take(new_in, destination_in, axis=0).reshape(shape_in)
    new_moment_a = jnp.take(new_moment_in, destination_in, axis=0).reshape(shape_in)
    new_weight_b = jnp.take(new_out, destination_out, axis=0).reshape(shape_out)
    new_moment_b = jnp.take(new_moment_out, destination_out, axis=0).reshape(shape_out)
    return (new_weight_a, new_weight_b, new_moment_a, new_moment_b)


def solution(mesh):
    placed = (
        P("replica", None, None, "shard"),
        P("replica", None, None, "shard"),
        P("replica", "section", None, "shard"),
        P("replica", "section", "shard", None),
        P("replica", "section", None, "shard"),
        P("replica", "section", "shard", None),
        P(),
        P(),
    )
    return jax.shard_map(
        per_device,
        mesh=mesh,
        in_specs=placed,
        out_specs=(
            P("replica", "section", None, "shard"),
            P("replica", "section", "shard", None),
            P("replica", "section", None, "shard"),
            P("replica", "section", "shard", None),
        ),
        check_vma=False,
    )
```

profile of v0, /device:TPU:32, one launch (start us, length us, event | category | flops | bytes accessed | tf_op | source)
XLA Modules:
  0.0 750.2 jit_solution(7037849973618554209)
XLA Ops:
  8.2 12.6 %all_gather.24 = bf16[128,1024]{1,0:T(8,128)(2,1)S(1)} all-gather(bf16[128,256]{1,0:T(8,128)(2,1)S(1)} %bitcast_select_fusion.6), channel_id=1, replica_groups=mesh['replica'=16,'section'=4,'shard'=4] {'shard'}, dimensions={1}, use_global_device_ids=true | all-gather | bytes 327680 | tf_op jit(solution)/shard_map/all_gather | solution.py:78
  20.9 1.8 fusion.74
  25.7 24.3 %reduce-scatter.8.cloned.1.call-done = bf16[128,256]{1,0:T(8,128)(2,1)} async-done(((bf16[128,1024]{1,0:T(8,128)(2,1)}), bf16[128,256]{1,0:T(8,128)(2,1)}) %reduce-scatter.8.cloned.1.call-update) | async-done | bytes 65552 | tf_op jit(solution)/shard_map/reduce_scatter | solution.py:84
  51.5 15.8 %all_to_all.60 = bf16[16,8,256]{2,1,0:T(8,128)(2,1)S(1)} all-to-all(bf16[16,8,256]{2,1,0:T(8,128)(2,1)S(1)} %broadcast_select_fusion.10), channel_id=1, replica_groups=mesh['replica'=16,'section'=4,'shard'=4] {'replica'}, dimensions={0} | all-to-all | bytes 131072 | tf_op jit(solution)/shard_map/all_to_all | solution.py:94
  69.5 12.3 %all_gather.25 = bf16[128,1024]{1,0:T(8,128)(2,1)S(1)} all-gather(bf16[128,256]{1,0:T(8,128)(2,1)S(1)} %bitcast_select_fusion.5), channel_id=1, replica_groups=mesh['replica'=16,'section'=4,'shard'=4] {'shard'}, dimensions={1}, use_global_device_ids=true | all-gather | bytes 327680 | tf_op jit(solution)/shard_map/all_gather | solution.py:78
  84.8 23.8 %reduce-scatter.10.cloned.1.call-done = bf16[128,256]{1,0:T(8,128)(2,1)} async-done(((bf16[128,1024]{1,0:T(8,128)(2,1)}), bf16[128,256]{1,0:T(8,128)(2,1)}) %reduce-scatter.10.cloned.1.call-update) | async-done | bytes 65552 | tf_op jit(solution)/shard_map/reduce_scatter | solution.py:84
  110.1 15.8 %all_to_all.61 = bf16[16,8,256]{2,1,0:T(8,128)(2,1)S(1)} all-to-all(bf16[16,8,256]{2,1,0:T(8,128)(2,1)S(1)} %broadcast_select_fusion.11), channel_id=1, replica_groups=mesh['replica'=16,'section'=4,'shard'=4] {'replica'}, dimensions={0} | all-to-all | bytes 131072 | tf_op jit(solution)/shard_map/all_to_all | solution.py:94
  128.1 12.3 %all_gather.26 = bf16[128,1024]{1,0:T(8,128)(2,1)S(1)} all-gather(bf16[128,256]{1,0:T(8,128)(2,1)S(1)} %bitcast_select_fusion.4), channel_id=1, replica_groups=mesh['replica'=16,'section'=4,'shard'=4] {'shard'}, dimensions={1}, use_global_device_ids=true | all-gather | bytes 327680 | tf_op jit(solution)/shard_map/all_gather | solution.py:78
  143.4 23.8 %reduce-scatter.12.cloned.1.call-done = bf16[128,256]{1,0:T(8,128)(2,1)} async-done(((bf16[128,1024]{1,0:T(8,128)(2,1)}), bf16[128,256]{1,0:T(8,128)(2,1)}) %reduce-scatter.12.cloned.1.call-update) | async-done | bytes 65552 | tf_op jit(solution)/shard_map/reduce_scatter | solution.py:84
  168.7 15.8 %all_to_all.62 = bf16[16,8,256]{2,1,0:T(8,128)(2,1)S(1)} all-to-all(bf16[16,8,256]{2,1,0:T(8,128)(2,1)S(1)} %broadcast_select_fusion.12), channel_id=1, replica_groups=mesh['replica'=16,'section'=4,'shard'=4] {'replica'}, dimensions={0} | all-to-all | bytes 131072 | tf_op jit(solution)/shard_map/all_to_all | solution.py:94
  187.4 12.2 %all_gather.27 = bf16[128,1024]{1,0:T(8,128)(2,1)S(1)} all-gather(bf16[128,256]{1,0:T(8,128)(2,1)S(1)} %bitcast_select_fusion.3), channel_id=1, replica_groups=mesh['replica'=16,'section'=4,'shard'=4] {'shard'}, dimensions={1}, use_global_device_ids=true | all-gather | bytes 327680 | tf_op jit(solution)/shard_map/all_gather | solution.py:78
  203.4 23.8 %reduce-scatter.14.cloned.1.call-done = bf16[128,256]{1,0:T(8,128)(2,1)} async-done(((bf16[128,1024]{1,0:T(8,128)(2,1)}), bf16[128,256]{1,0:T(8,128)(2,1)}) %reduce-scatter.14.cloned.1.call-update) | async-done | bytes 65552 | tf_op jit(solution)/shard_map/reduce_scatter | solution.py:84
  228.3 12.3 %all_gather.28 = bf16[128,1024]{1,0:T(8,128)(2,1)S(1)} all-gather(bf16[128,256]{1,0:T(8,128)(2,1)S(1)} %get-tuple-element.15), channel_id=1, replica_groups=mesh['replica'=16,'section'=4,'shard'=4] {'shard'}, dimensions={1}, use_global_device_ids=true | all-gather | bytes 327680 | tf_op jit(solution)/shard_map/all_gather | solution.py:130
  240.6 1.8 fusion.131
  244.4 23.0 %reduce-scatter.16.cloned.1.call-done = bf16[128,256]{1,0:T(8,128)(2,1)} async-done(((bf16[128,1024]{1,0:T(8,128)(2,1)}), bf16[128,256]{1,0:T(8,128)(2,1)}) %reduce-scatter.16.cloned.1.call-update) | async-done | bytes 65552 | tf_op jit(solution)/shard_map/reduce_scatter | solution.py:160
  268.5 9.1 %psum.21 = f32[128]{0:T(128)} all-reduce(f32[128]{0:T(128)S(1)} %fusion.160), channel_id=1, replica_groups=mesh['replica'=16,'section'=4,'shard'=4] {'shard'}, use_global_device_ids=true, to_apply=%region_13.16 | all-reduce | flops 128 | bytes 1024 | tf_op jit(solution)/shard_map/psum | solution.py:167
  279.8 8.4 %all-to-all-start.5 = ((bf16[16,8,256]{2,1,0:T(8,128)(2,1)}), bf16[16,8,256]{2,1,0:T(8,128)(2,1)S(1)}, u32[]{:S(2)}, u32[]{:S(2)}) async-start(bf16[16,8,256]{2,1,0:T(8,128)(2,1)} %fusion.176), calls=%async_computation.10 | async-start | bytes 131072 | tf_op jit(solution)/shard_map/all_to_all | solution.py:174
  288.8 7.1 all-to-all-done.5
  299.1 2.0 gather_fusion.5
  302.1 12.3 %all_gather.29 = bf16[128,1024]{1,0:T(8,128)(2,1)S(1)} all-gather(bf16[128,256]{1,0:T(8,128)(2,1)S(1)} %fusion.179), channel_id=1, replica_groups=mesh['replica'=16,'section'=4,'shard'=4] {'shard'}, dimensions={1}, use_global_device_ids=true | all-gather | bytes 327680 | tf_op jit(solution)/shard_map/all_gather | solution.py:130
  320.8 17.0 %reduce-scatter.18.cloned.1.call-done = bf16[128,256]{1,0:T(8,128)(2,1)} async-done(((bf16[128,1024]{1,0:T(8,128)(2,1)}), bf16[128,256]{1,0:T(8,128)(2,1)}) %reduce-scatter.18.cloned.1.call-update) | async-done | bytes 65552 | tf_op jit(solution)/shard_map/reduce_scatter | solution.py:160
  338.8 9.1 %psum.22 = f32[128]{0:T(128)} all-reduce(f32[128]{0:T(128)S(1)} %fusion.164), channel_id=1, replica_groups=mesh['replica'=16,'section'=4,'shard'=4] {'shard'}, use_global_device_ids=true, to_apply=%region_16.19 | all-reduce | flops 128 | bytes 1024 | tf_op jit(solution)/shard_map/psum | solution.py:167
  350.1 8.4 %all-to-all-start.6 = ((bf16[16,8,256]{2,1,0:T(8,128)(2,1)}), bf16[16,8,256]{2,1,0:T(8,128)(2,1)S(1)}, u32[]{:S(2)}, u32[]{:S(2)}) async-start(bf16[16,8,256]{2,1,0:T(8,128)(2,1)} %fusion.175), calls=%async_computation.12 | async-start | bytes 131072 | tf_op jit(solution)/shard_map/all_to_all | solution.py:174
  359.6 6.5 all-to-all-done.6
  368.1 1.8 gather_fusion.10
  369.8 3.2 gather_fusion.11
  373.0 2.0 gather_fusion.6
  376.0 12.5 %all_gather.30 = bf16[128,1024]{1,0:T(8,128)(2,1)S(1)} all-gather(bf16[128,256]{1,0:T(8,128)(2,1)S(1)} %fusion.178), channel_id=1, replica_groups=mesh['replica'=16,'section'=4,'shard'=4] {'shard'}, dimensions={1}, use_global_device_ids=true | all-gather | bytes 327680 | tf_op jit(solution)/shard_map/all_gather | solution.py:130
  393.5 3.3 fusion.199
  396.7 14.9 %reduce-scatter.20.cloned.1.call-done = bf16[128,256]{1,0:T(8,128)(2,1)} async-done(((bf16[128,1024]{1,0:T(8,128)(2,1)}), bf16[128,256]{1,0:T(8,128)(2,1)}) %reduce-scatter.20.cloned.1.call-update) | async-done | bytes 65552 | tf_op jit(solution)/shard_map/reduce_scatter | solution.py:160
  413.2 9.2 %psum.23 = f32[128]{0:T(128)} all-reduce(f32[128]{0:T(128)} %fusion.168), channel_id=1, replica_groups=mesh['replica'=16,'section'=4,'shard'=4] {'shard'}, use_global_device_ids=true, to_apply=%region_19.22 | all-reduce | flops 128 | bytes 1024 | tf_op jit(solution)/shard_map/psum | solution.py:167
  424.6 8.4 %all-to-all-start.7 = ((bf16[16,8,256]{2,1,0:T(8,128)(2,1)}), bf16[16,8,256]{2,1,0:T(8,128)(2,1)S(1)}, u32[]{:S(2)}, u32[]{:S(2)}) async-start(bf16[16,8,256]{2,1,0:T(8,128)(2,1)} %fusion.174), calls=%async_computation.14 | async-start | bytes 131072 | tf_op jit(solution)/shard_map/all_to_all | solution.py:174
  433.0 3.3 fusion.200
  436.3 4.3 all-to-all-done.7
  442.1 3.4 fusion.201
  445.5 2.0 gather_fusion.7
  448.4 12.5 %all_gather.31 = bf16[128,1024]{1,0:T(8,128)(2,1)S(1)} all-gather(bf16[128,256]{1,0:T(8,128)(2,1)S(1)} %fusion.177), channel_id=1, replica_groups=mesh['replica'=16,'section'=4,'shard'=4] {'shard'}, dimensions={1}, use_global_device_ids=true | all-gather | bytes 327680 | tf_op jit(solution)/shard_map/all_gather | solution.py:130
  460.9 5.7 multiply_convert_fusion
  466.6 3.2 gather_fusion.12
  469.8 4.0 broadcast_select_fusion.3
  473.8 41.9 %all_to_all.63 = bf16[16,48,1024]{2,1,0:T(8,128)(2,1)} all-to-all(bf16[16,48,1024]{2,1,0:T(8,128)(2,1)S(1)} %get-tuple-element.26), channel_id=1, replica_groups=mesh['replica'=16,'section'=4,'shard'=4] {'replica'}, dimensions={0} | all-to-all | bytes 3145728 | tf_op jit(solution)/shard_map/all_to_all | solution.py:184
  515.7 42.3 %all_to_all.64 = bf16[16,48,1024]{2,1,0:T(8,128)(2,1)} all-to-all(bf16[16,48,1024]{2,1,0:T(8,128)(2,1)S(1)} %get-tuple-element.27), channel_id=1, replica_groups=mesh['replica'=16,'section'=4,'shard'=4] {'replica'}, dimensions={0} | all-to-all | bytes 3145728 | tf_op jit(solution)/shard_map/all_to_all | solution.py:185
  558.0 5.3 all-to-all-start.9
  563.4 1.8 gather_fusion
  565.2 3.2 gather_fusion.1
  568.5 2.3 fusion.195
  570.8 2.3 fusion.193
  573.2 2.4 fusion.191
  575.6 5.2 multiply_convert_fusion.1
  580.7 1.8 gather_fusion.8
  582.5 4.0 broadcast_select_fusion.8
  586.5 13.3 %all-to-all-done.9 = bf16[16,48,1024]{2,1,0:T(8,128)(2,1)} async-done(((bf16[16,48,1024]{2,1,0:T(8,128)(2,1)}), bf16[16,48,1024]{2,1,0:T(8,128)(2,1)}, u32[]{:S(2)}, u32[]{:S(2)}) %all-to-all-start.9) | async-done | bytes 1572896 | tf_op jit(solution)/shard_map/all_to_all | solution.py:183
  599.8 42.5 %all_to_all.65 = bf16[16,64,768]{2,1,0:T(8,128)(2,1)} all-to-all(bf16[16,64,768]{2,1,0:T(8,128)(2,1)S(1)} %get-tuple-element.31), channel_id=1, replica_groups=mesh['replica'=16,'section'=4,'shard'=4] {'replica'}, dimensions={0} | all-to-all | bytes 3145728 | tf_op jit(solution)/shard_map/all_to_all | solution.py:180
  642.3 42.1 %all_to_all.66 = bf16[16,64,768]{2,1,0:T(8,128)(2,1)} all-to-all(bf16[16,64,768]{2,1,0:T(8,128)(2,1)S(1)} %get-tuple-element.29), channel_id=1, replica_groups=mesh['replica'=16,'section'=4,'shard'=4] {'replica'}, dimensions={0} | all-to-all | bytes 3145728 | tf_op jit(solution)/shard_map/all_to_all | solution.py:181
  684.4 5.4 all-to-all-start.8
  689.9 7.1 fusion.1
  697.0 3.2 gather_fusion.13
  700.2 3.4 gather_fusion.15
  703.7 22.5 %all-to-all-done.8 = bf16[16,64,768]{2,1,0:T(8,128)(2,1)} async-done(((bf16[16,64,768]{2,1,0:T(8,128)(2,1)}), bf16[16,64,768]{2,1,0:T(8,128)(2,1)}, u32[]{:S(2)}, u32[]{:S(2)}) %all-to-all-start.8) | async-done | bytes 1572896 | tf_op jit(solution)/shard_map/all_to_all | solution.py:182
  726.2 6.5 fusion
  732.7 3.3 gather_fusion.9
  736.0 1.8 gather_fusion.14
  737.8 3.6 broadcast_select_fusion
  741.4 2.0 broadcast_select_fusion.5
  (183 shorter events, 61.6 us)
Async XLA Ops:
  7.2 16.4 %copy-start = (bf16[1,1,768,1024]{3,2,1,0:T(8,128)(2,1)S(1)}, bf16[1,1,768,1024]{3,2,1,0:T(8,128)(2,1)}, u32[]{:S(2)}) copy-start(bf16[1,1,768,1024]{3,2,1,0:T(8,128)(2,1)} %param.17) | copy-start | bytes 4718596
  7.2 42.8 %reduce-scatter.8.cloned.1.call-start = ((), (), s32[]{:S(2)}) async-start(), calls=%async_computation.19 | async-start | bytes 327680 | tf_op jit(solution)/shard_map/reduce_scatter | solution.py:84
  20.8 2.0 copy-start.15
  22.8 0.7 copy-start.34
  23.5 26.4 %copy-start.18 = (bf16[1,1,128,256]{3,2,1,0:T(8,128)(2,1)S(1)}, bf16[1,1,128,256]{3,2,1,0:T(8,128)(2,1)}, u32[]{:S(2)}) copy-start(bf16[1,1,128,256]{3,2,1,0:T(8,128)(2,1)} %param.14) | copy-start | bytes 196612
  24.6 57.8 %copy-start.2 = (bf16[1,1,1024,768]{3,2,1,0:T(8,128)(2,1)S(1)}, bf16[1,1,1024,768]{3,2,1,0:T(8,128)(2,1)}, u32[]{:S(2)}) copy-start(bf16[1,1,1024,768]{3,2,1,0:T(8,128)(2,1)} %param.16) | copy-start | bytes 4718596
  24.6 84.0 %reduce-scatter.10.cloned.1.call-start = ((), (), s32[]{:S(2)}) async-start(), calls=%async_computation.20 | async-start | bytes 327680 | tf_op jit(solution)/shard_map/reduce_scatter | solution.py:84
  67.3 2.2 collective-permute-start
  69.5 39.1 %copy-start.20 = (bf16[128,256]{1,0:T(8,128)(2,1)}, bf16[128,256]{1,0:T(8,128)(2,1)S(1)}, u32[]{:S(2)}) copy-start(bf16[128,256]{1,0:T(8,128)(2,1)S(1)} %bitcast_select_fusion.5) | copy-start | bytes 196612
  81.8 0.7 copy-start.16
  82.9 0.7 copy-start.36
  84.8 82.4 %reduce-scatter.12.cloned.1.call-start = ((), (), s32[]{:S(2)}) async-start(), calls=%async_computation.21 | async-start | bytes 327680 | tf_op jit(solution)/shard_map/reduce_scatter | solution.py:84
  125.9 2.2 collective-permute-start.1
  128.1 39.1 %copy-start.21 = (bf16[128,256]{1,0:T(8,128)(2,1)}, bf16[128,256]{1,0:T(8,128)(2,1)S(1)}, u32[]{:S(2)}) copy-start(bf16[128,256]{1,0:T(8,128)(2,1)S(1)} %bitcast_select_fusion.4) | copy-start | bytes 196612
  140.4 0.7 copy-start.17
  141.5 0.7 copy-start.38
  143.4 83.8 %reduce-scatter.14.cloned.1.call-start = ((), (), s32[]{:S(2)}) async-start(), calls=%async_computation.22 | async-start | bytes 327680 | tf_op jit(solution)/shard_map/reduce_scatter | solution.py:84
  184.6 2.2 collective-permute-start.2
  185.9 15.0 %copy-start.35 = (f32[128,768]{1,0:T(8,128)S(1)}, f32[128,768]{1,0:T(8,128)}, u32[]{:S(2)}) copy-start(f32[128,768]{1,0:T(8,128)} %copy-done.34) | copy-start | bytes 1179652
  185.9 15.0 %copy-start.37 = (f32[128,768]{1,0:T(8,128)S(1)}, f32[128,768]{1,0:T(8,128)}, u32[]{:S(2)}) copy-start(f32[128,768]{1,0:T(8,128)} %copy-done.36) | copy-start | bytes 1179652
  185.9 15.0 %copy-start.39 = (f32[128,768]{1,0:T(8,128)S(1)}, f32[128,768]{1,0:T(8,128)}, u32[]{:S(2)}) copy-start(f32[128,768]{1,0:T(8,128)} %copy-done.38) | copy-start | bytes 1179652
  186.7 0.6 copy-start.31
  203.3 64.1 %reduce-scatter.16.cloned.1.call-start = ((), (), s32[]{:S(2)}) async-start(), calls=%async_computation.23 | async-start | bytes 327680 | tf_op jit(solution)/shard_map/reduce_scatter | solution.py:160
  228.3 12.3 %copy-start.32 = (bf16[128,256]{1,0:T(8,128)(2,1)}, bf16[128,256]{1,0:T(8,128)(2,1)S(1)}, u32[]{:S(2)}) copy-start(bf16[128,256]{1,0:T(8,128)(2,1)S(1)} %get-tuple-element.15) | copy-start | bytes 196612
  240.6 1.8 copy-start.22
  242.3 0.7 copy-start.25
  243.0 35.2 %copy-start.33 = (bf16[128,256]{1,0:T(8,128)(2,1)S(1)}, bf16[128,256]{1,0:T(8,128)(2,1)}, u32[]{:S(2)}) copy-start(bf16[128,256]{1,0:T(8,128)(2,1)} %copy-done.32) | copy-start | bytes 196612
  279.8 16.0 %all-to-all-start.5 = ((bf16[16,8,256]{2,1,0:T(8,128)(2,1)}), bf16[16,8,256]{2,1,0:T(8,128)(2,1)S(1)}, u32[]{:S(2)}, u32[]{:S(2)}) async-start(bf16[16,8,256]{2,1,0:T(8,128)(2,1)} %fusion.176), calls=%async_computation.10 | async-start | bytes 131072 | tf_op jit(solution)/shard_map/all_to_all | solution.py:174
  288.2 49.5 %reduce-scatter.18.cloned.1.call-start = ((), (), s32[]{:S(2)}) async-start(), calls=%async_computation.24 | async-start | bytes 327680 | tf_op jit(solution)/shard_map/reduce_scatter | solution.py:160
  295.8 3.3 collective-permute-start.3
  314.3 1.8 copy-start.23
  316.1 0.7 copy-start.27
  319.6 0.6 copy-start.43
  350.1 16.0 %all-to-all-start.6 = ((bf16[16,8,256]{2,1,0:T(8,128)(2,1)}), bf16[16,8,256]{2,1,0:T(8,128)(2,1)S(1)}, u32[]{:S(2)}, u32[]{:S(2)}) async-start(bf16[16,8,256]{2,1,0:T(8,128)(2,1)} %fusion.175), calls=%async_computation.12 | async-start | bytes 131072 | tf_op jit(solution)/shard_map/all_to_all | solution.py:174
  358.5 53.2 %reduce-scatter.20.cloned.1.call-start = ((), (), s32[]{:S(2)}) async-start(), calls=%async_computation.25 | async-start | bytes 327680 | tf_op jit(solution)/shard_map/reduce_scatter | solution.py:160
  366.1 6.9 collective-permute-start.4
  388.4 1.8 copy-start.24
  390.2 0.7 copy-start.29
  424.6 16.0 %all-to-all-start.7 = ((bf16[16,8,256]{2,1,0:T(8,128)(2,1)}), bf16[16,8,256]{2,1,0:T(8,128)(2,1)S(1)}, u32[]{:S(2)}, u32[]{:S(2)}) async-start(bf16[16,8,256]{2,1,0:T(8,128)(2,1)} %fusion.174), calls=%async_computation.14 | async-start | bytes 131072 | tf_op jit(solution)/shard_map/all_to_all | solution.py:174
  440.6 4.8 collective-permute-start.5
  460.9 5.7 copy-start.19
  466.6 3.2 copy-start.41
  473.8 41.9 %copy-start.3 = (bf16[16,48,1024]{2,1,0:T(8,128)(2,1)}, bf16[16,48,1024]{2,1,0:T(8,128)(2,1)S(1)}, u32[]{:S(2)}) copy-start(bf16[16,48,1024]{2,1,0:T(8,128)(2,1)S(1)} %get-tuple-element.26) | copy-start | bytes 4718596
  473.8 41.9 %copy-start.5 = (bf16[16,48,1024]{2,1,0:T(8,128)(2,1)}, bf16[16,48,1024]{2,1,0:T(8,128)(2,1)S(1)}, u32[]{:S(2)}) copy-start(bf16[16,48,1024]{2,1,0:T(8,128)(2,1)S(1)} %get-tuple-element.27) | copy-start | bytes 4718596
  558.0 5.3 copy-start.42
  558.0 41.8 %all-to-all-start.9 = ((bf16[16,48,1024]{2,1,0:T(8,128)(2,1)}), bf16[16,48,1024]{2,1,0:T(8,128)(2,1)}, u32[]{:S(2)}, u32[]{:S(2)}) async-start(bf16[16,48,1024]{2,1,0:T(8,128)(2,1)} %get-tuple-element.28), calls=%async_computation.16 | async-start | bytes 3145728 | tf_op jit(solution)/shard_map/all_to_all | solution.py:183
  565.2 3.3 copy-start.26
  568.5 2.3 copy-start.28
  570.8 2.4 copy-start.30
  586.5 55.8 %copy-start.10 = (bf16[16,64,768]{2,1,0:T(8,128)(2,1)}, bf16[16,64,768]{2,1,0:T(8,128)(2,1)S(1)}, u32[]{:S(2)}) copy-start(bf16[16,64,768]{2,1,0:T(8,128)(2,1)S(1)} %get-tuple-element.31) | copy-start | bytes 4718596
  586.5 55.8 %copy-start.7 = (bf16[16,64,768]{2,1,0:T(8,128)(2,1)}, bf16[16,64,768]{2,1,0:T(8,128)(2,1)S(1)}, u32[]{:S(2)}) copy-start(bf16[16,64,768]{2,1,0:T(8,128)(2,1)S(1)} %get-tuple-element.29) | copy-start | bytes 4718596
  642.3 47.6 %copy-start.44 = (s32[16]{0:T(128)S(1)}, s32[16]{0:T(128)}, u32[]{:S(2)}) copy-start(s32[16]{0:T(128)} %copy-done.43) | copy-start | bytes 196
  684.4 5.5 copy-start.4
  684.4 5.5 copy-start.6
  684.4 41.8 %all-to-all-start.8 = ((bf16[16,64,768]{2,1,0:T(8,128)(2,1)}), bf16[16,64,768]{2,1,0:T(8,128)(2,1)}, u32[]{:S(2)}, u32[]{:S(2)}) async-start(bf16[16,64,768]{2,1,0:T(8,128)(2,1)} %get-tuple-element.30), calls=%async_computation.15 | async-start | bytes 3145728 | tf_op jit(solution)/shard_map/all_to_all | solution.py:182
  700.2 25.9 %copy-start.8 = (bf16[16,64,768]{2,1,0:T(8,128)(2,1)S(1)}, bf16[16,64,768]{2,1,0:T(8,128)(2,1)}, u32[]{:S(2)}) copy-start(bf16[16,64,768]{2,1,0:T(8,128)(2,1)} %copy-done.7) | copy-start | bytes 4718596
  700.2 25.9 %copy-start.9 = (bf16[16,64,768]{2,1,0:T(8,128)(2,1)S(1)}, bf16[16,64,768]{2,1,0:T(8,128)(2,1)}, u32[]{:S(2)}) copy-start(bf16[16,64,768]{2,1,0:T(8,128)(2,1)} %get-tuple-element.30) | copy-start | bytes 4718596
  732.6 3.3 copy-start.11
  736.0 1.8 copy-start.12
  736.0 1.8 copy-start.40
  737.8 3.6 copy-start.13
  737.8 3.6 copy-start.14
  741.3 2.0 copy-start.1
Sparse Core Ops, SparseCore 0:
  24.8 25.1 reduce-scatter.7
  84.9 23.6 reduce-scatter.9
  143.5 23.6 reduce-scatter.11
  203.4 23.6 reduce-scatter.13
  244.5 22.8 reduce-scatter.15
  318.3 19.4 reduce-scatter.17
  392.4 19.2 reduce-scatter.19
where the time goes:
time: 752 us; the launch traced here: 750 us
  blocking collectives  342 us (45%)
  waiting for transfers between devices  208 us (28%)
  other arithmetic  52.7 us (7%)
  matrix products  45.5 us (6%)
  starting transfers between devices  44.1 us (6%)
  local copies, waits for them, and re-layouts  42.6 us (6%)
  between operations  14.8 us (2%)
    reduce_scatter x7, waiting for transfers between devices, per_device(): lax.psum_scatter(term.astype(jnp.bfloat16), 'shard', scatter_dimension=1,...  151 us
    all_gather x4, blocking collectives, per_device(): gathered_up = lax.all_gather(upstream, 'shard', axis=1, tiled=True)  49.5 us
    all_gather x4, blocking collectives, per_device(): gathered = lax.all_gather(current, 'shard', axis=1, tiled=True)  49.4 us
    all_to_all x3, blocking collectives, per_device(): lax.all_to_all(send_grouped, 'replica', split_axis=0, concat_axis=0, tile...  47.5 us
    all_to_all x1, blocking collectives, per_device(): lax.all_to_all(state_in, 'replica', split_axis=0, concat_axis=0, tiled=True)  42.5 us
    all_to_all x1, blocking collectives, per_device(): lax.all_to_all(delta_out, 'replica', split_axis=0, concat_axis=0, tiled=T...  42.3 us
    all_to_all x1, blocking collectives, per_device(): lax.all_to_all(moment_in, 'replica', split_axis=0, concat_axis=0, tiled=T...  42.1 us
    all_to_all x1, blocking collectives, per_device(): lax.all_to_all(moment_out, 'replica', split_axis=0, concat_axis=0, tiled=...  41.9 us
  transfers between devices with their start and end apart: 18, of which 16 were waited for; matrix products, arithmetic and copies ran while one was open for 8% of the time, Pallas kernels for 0%

commit v1 on v0

v1 whole, which is shorter than its diff:
```python
import functools
import math

import jax
import jax.numpy as jnp
from jax import lax
from jax.experimental import pallas as pl
from jax.experimental.pallas import tpu as pltpu
from jax.sharding import PartitionSpec as P

MESH = pl.DeviceIdType.MESH
f32 = jnp.float32
bf16 = jnp.bfloat16

epsilon = 1e-05
inner_rate = 0.5
momentum_decay = 0.9
outer_rate = 0.7

step_size = outer_rate * (1.0 + momentum_decay)
mix_rate = step_size * momentum_decay - outer_rate * momentum_decay * momentum_decay

REPLICAS = 16
SECTIONS = 4
SHARDS = 4
ROWS = 128
GROUP = ROWS // REPLICAS
WIDTH = 1024
FEATURES = WIDTH // SHARDS
HIDDEN = 768
PIECE_A = WIDTH // REPLICAS
PIECE_B = HIDDEN // REPLICAS
scale_in = 1.0 / math.sqrt(WIDTH)
scale_out = 1.0 / math.sqrt(HIDDEN * SHARDS)

NN = (((1,), (0,)), ((), ()))
NT = (((1,), (1,)), ((), ()))


def dot(a, b, dims=NN):
    return lax.dot_general(a, b, dims, preferred_element_type=f32)


def pack_rows(wide):
    return jnp.concatenate([wide[:, :, :128], wide[:, :, 128:]], axis=1).astype(bf16)


def unpack_rows(packed):
    wide = packed.astype(f32)
    count = wide.shape[0]
    return jnp.concatenate(
        [
            wide[:, :GROUP, :].reshape(count * GROUP, 128),
            wide[:, GROUP:, :].reshape(count * GROUP, 128),
        ],
        axis=1,
    )


def kernel(
    inp_h, tgt_h, wa_h, wb_h, ma_h, mb_h, routes, partners,
    nwa_h, nwb_h, nma_h, nmb_h,
    inp, tgt, wa, wb, ma, mb,
    fwd_all, fwd_term, fwd_got, fwd_out, fwd_send, fwd_recv,
    bwd_all, bwd_term, bwd_got, bwd_send, bwd_recv, along_send, along_got, up_own,
    inv_rms, slope, hidden_t, normed_t, grad_pre, grad_a, grad_b,
    qa_send, qb_send, qa_recv, qb_recv, va_send, vb_send, va_recv, vb_recv,
    order_f, order_a, order_b,
    load_sem, store_sem, x_send, x_recv, z_send, z_recv, bulk_send, bulk_recv,
):
    r = lax.axis_index("replica")
    s = lax.axis_index("section")
    x = lax.axis_index("shard")
    y, z = r // 8, lax.rem(r, 8)
    first, last = s == 0, s == SECTIONS - 1

    def other_shard(d):
        return lax.rem(x + d, SHARDS)

    def peer(t):
        dy, h = lax.rem(t, 2), t // 2
        odd = lax.rem(h, 2)
        dz = odd * ((h + 1) // 2) + (1 - odd) * lax.rem(8 - h // 2, 8)
        return lax.rem(y + dy, 2) * 8 + lax.rem(z + dz, 8)

    def each(count, body, start=0):
        def step(i, carry):
            body(i)
            return carry

        lax.fori_loop(start, count, step, 0)

    loads = [
        pltpu.make_async_copy(src, dst, load_sem.at[i])
        for i, (src, dst) in enumerate(
            [(inp_h, inp), (wa_h, wa), (wb_h, wb), (ma_h, ma), (mb_h, mb), (tgt_h, tgt)]
        )
    ]
    for copy in loads:
        copy.start()

    barrier = pltpu.get_barrier_semaphore()

    def greet(device):
        pl.semaphore_signal(barrier, inc=1, device_id=device, device_id_type=MESH)

    for d in (1, 2, 3):
        greet((r, s, other_shard(d)))

    @pl.when(s < SECTIONS - 1)
    def _():
        each(REPLICAS, lambda t: greet((peer(t), s + 1, x)))

    @pl.when(s > 0)
    def _():
        each(REPLICAS, lambda t: greet((peer(t), s - 1, x)))

    each(REPLICAS, lambda t: greet((peer(t), s, x)), 1)

    links = jnp.minimum(s, 1) + jnp.minimum(SECTIONS - 1 - s, 1)
    pl.semaphore_wait(barrier, SHARDS - 1 + REPLICAS - 1 + REPLICAS * links)


    def gather_copy(ref, phase, d):
        return pltpu.make_async_remote_copy(
            ref.at[x], ref.at[x], x_send.at[phase, d], x_recv.at[phase, d],
            device_id=(r, s, other_shard(d)), device_id_type=MESH,
        )

    def scatter_copy(src, dst, phase, d):
        return pltpu.make_async_remote_copy(
            src.at[other_shard(d)], dst.at[x], x_send.at[phase, d], x_recv.at[phase, d],
            device_id=(r, s, other_shard(d)), device_id_type=MESH,
        )

    def route_copy(src, slot, dst, phase, t, section):
        return pltpu.make_async_remote_copy(
            src.at[slot], dst.at[r], z_send.at[phase], z_recv.at[phase],
            device_id=(peer(t), section, x), device_id_type=MESH,
        )

    def route_wait_recv(dst, phase):
        pltpu.make_async_copy(dst, dst, z_recv.at[phase]).wait()

    def route_wait_send(src, phase):
        pltpu.make_async_copy(src, src, z_send.at[phase]).wait()

    def bulk_start(src, dst, which):
        def body(t):
            p = peer(t)
            pltpu.make_async_remote_copy(
                src.at[p], dst.at[r], bulk_send.at[which], bulk_recv.at[which],
                device_id=(p, s, x), device_id_type=MESH,
            ).start()

        each(REPLICAS, body, 1)

    def bulk_wait_recv(dst, which):
        part = dst.at[0 : REPLICAS - 1]
        pltpu.make_async_copy(part, part, bulk_recv.at[which]).wait()

    def bulk_wait_send(src, which):
        part = src.at[0 : REPLICAS - 1]
        pltpu.make_async_copy(part, part, bulk_send.at[which]).wait()


    def invert(table, out):
        def body(p):
            found = 0
            for g in range(REPLICAS):
                apart = table(g) - p
                found = jnp.maximum(found, g * (1 - jnp.minimum(apart * apart, 1)))
            out[p] = found

        each(REPLICAS, body)

    link = jnp.minimum(s, SECTIONS - 2)


    def fill_q(w, m, order, send, recv):
        def body(p):
            k = order[p]
            value = (w[k].astype(f32) + mix_rate * m[k].astype(f32)).astype(bf16)
            send[p] = value

        each(REPLICAS, body)
        recv[r] = send[r]

    def fill_v(m, grad, factor, order, send, recv):
        def body(p):
            k = order[p]
            value = momentum_decay * m[k].astype(f32) + factor * grad[k]
            send[p] = value.astype(bf16)

        each(REPLICAS, body)
        recv[r] = send[r]

    def prepare_q():
        invert(lambda g: partners[s, 0, g, r], order_a)
        invert(lambda g: partners[s, 1, g, r], order_b)
        loads[3].wait()
        loads[4].wait()
        fill_q(wb, mb, order_b, qb_send, qb_recv)
        fill_q(wa, ma, order_a, qa_send, qa_recv)

    def rows_a(j):
        span = FEATURES // PIECE_A
        return wa[pl.ds(j * span, span)].reshape(FEATURES, HIDDEN)

    def columns_b(j):
        columns = pl.ds(pl.multiple_of(j * FEATURES, FEATURES), FEATURES)
        return wb[:, :, columns].reshape(HIDDEN, FEATURES)


    loads[0].wait()

    @pl.when(first)
    def _():
        fwd_all[x] = inp[...]

    @pl.when(s > 0)
    def _():
        loads[1].wait()
        loads[2].wait()
        prepare_q()

    @pl.when(s >= 2)
    def _():
        bulk_start(qb_send, qb_recv, 0)

    @pl.when(last)
    def _():
        bulk_start(qa_send, qa_recv, 1)

    @pl.when(s > 0)
    def _():
        invert(lambda g: routes[link, r, g], order_f)
        route_wait_recv(fwd_recv, 0)
        fwd_all[x] = unpack_rows(fwd_recv[...]).astype(bf16)

    for d in (2, 1, 3):
        gather_copy(fwd_all, 0, d).start()

    @pl.when(first)
    def _():
        invert(lambda g: routes[link, r, g], order_f)
        loads[1].wait()
        loads[2].wait()

    preact = jnp.zeros((ROWS, HIDDEN), f32)
    square = jnp.zeros((ROWS, 1), f32)
    for d in (0, 1, 3, 2):
        if d:
            gather_copy(fwd_all, 0, d).wait_recv()
        j = lax.rem(x + SHARDS - d, SHARDS)
        part = fwd_all[j]
        preact = preact + dot(part, rows_a(j))
        wide = part.astype(f32)
        square = square + jnp.sum(wide * wide, axis=1, keepdims=True)
    inverse = lax.rsqrt(square * (1.0 / WIDTH) + epsilon)
    inv_rms[...] = jnp.broadcast_to(inverse, inv_rms.shape)
    preact = preact * (inverse * scale_in)
    gate = 1.0 / (1.0 + jnp.exp(-preact))
    hidden = (preact * gate).astype(bf16)
    slope[...] = (gate * (1.0 + preact * (1.0 - gate))) * scale_out
    for d in (2, 1, 3, 0):
        j = other_shard(d)
        fwd_term[j] = (dot(hidden, columns_b(j)) * scale_out).astype(bf16)
        if d:
            scatter_copy(fwd_term, fwd_got, 1, d).start()
    total = fwd_term[x].astype(f32)
    for d in (1, 3, 2):
        scatter_copy(fwd_term, fwd_got, 1, d).wait_recv()
        total = total + fwd_got[lax.rem(x + SHARDS - d, SHARDS)].astype(f32)
    output = (fwd_all[x].astype(f32) + total).astype(bf16).astype(f32)

    @pl.when(s < SECTIONS - 1)
    def _():
        fwd_out[...] = output.reshape(REPLICAS, GROUP, FEATURES)
        for t in range(REPLICAS - 1, -1, -1):
            block = fwd_out[order_f[peer(t)]]
            fwd_send[t] = pack_rows(block[None])[0]
            route_copy(fwd_send, t, fwd_recv, 0, t, s + 1).start()

    @pl.when(last)
    def _():
        loads[5].wait()
        up = (output - tgt[...].astype(f32)).astype(bf16)
        bwd_all[x] = up
        up_own[...] = up.astype(f32)
        for d in (2, 1, 3):
            gather_copy(bwd_all, 2, d).start()


    @pl.when(first)
    def _():
        prepare_q()
        bulk_start(qb_send, qb_recv, 0)

    @pl.when(s == 1)
    def _():
        bulk_start(qb_send, qb_recv, 0)

    @pl.when(s < SECTIONS - 1)
    def _():
        loads[5].wait()
        bulk_start(qa_send, qa_recv, 1)

    hidden_t[...] = hidden.T
    for j in range(SHARDS):
        normed = (fwd_all[j].astype(f32) * inverse).astype(bf16)
        normed_t[j * FEATURES : (j + 1) * FEATURES, :] = normed.T


    @pl.when(s < SECTIONS - 1)
    def _():
        route_wait_recv(bwd_recv, 1)
        for g in range(REPLICAS):
            block = bwd_recv[routes[link, r, g]]
            up_own[g * GROUP : (g + 1) * GROUP, :] = unpack_rows(block[None])
        bwd_all[x] = up_own[...].astype(bf16)
        for d in (2, 1, 3):
            gather_copy(bwd_all, 2, d).start()

    grad_hidden = jnp.zeros((ROWS, HIDDEN), f32)
    for d in (0, 1, 3, 2):
        if d:
            gather_copy(bwd_all, 2, d).wait_recv()
        j = lax.rem(x + SHARDS - d, SHARDS)
        grad_hidden = grad_hidden + dot(bwd_all[j], columns_b(j), NT)
    grad_pre[...] = (grad_hidden * slope[...]).astype(bf16)

    def outer_b():
        for j in range(SHARDS):
            value = dot(hidden_t[...], bwd_all[j]).reshape(REPLICAS, PIECE_B, FEATURES)
            grad_b[:, :, j * FEATURES : (j + 1) * FEATURES] = value
        fill_v(mb, grad_b, inner_rate * scale_out, order_b, vb_send, vb_recv)
        bulk_start(vb_send, vb_recv, 2)

    def outer_a():
        for j in range(SHARDS):
            value = dot(normed_t[j * FEATURES : (j + 1) * FEATURES, :], grad_pre[...])
            span = FEATURES // PIECE_A
            grad_a[j * span : (j + 1) * span] = value.reshape(span, PIECE_A, HIDDEN)
        fill_v(ma, grad_a, inner_rate * scale_in, order_a, va_send, va_recv)
        bulk_start(va_send, va_recv, 3)

    @pl.when(s > 0)
    def _():
        inverse = inv_rms[:, :1]
        share = jnp.zeros((ROWS, 1), f32)
        for d in (2, 1, 3, 0):
            j = other_shard(d)
            term = (dot(grad_pre[...], rows_a(j), NT) * scale_in).astype(bf16)
            bwd_term[j] = term
            if d:
                scatter_copy(bwd_term, bwd_got, 3, d).start()
            exact = fwd_all[j].astype(f32) * inverse
            share = share + jnp.sum(term.astype(f32) * exact, axis=1, keepdims=True)
        diagonal = lax.broadcasted_iota(jnp.int32, (ROWS, ROWS), 0) == lax.broadcasted_iota(
            jnp.int32, (ROWS, ROWS), 1
        )
        row = jnp.sum(jnp.where(diagonal, share, 0.0), axis=0, keepdims=True)
        along_send[...] = jnp.broadcast_to(row, along_send.shape)

        def along_copy(d):
            return pltpu.make_async_remote_copy(
                along_send, along_got.at[x], x_send.at[4, d], x_recv.at[4, d],
                device_id=(r, s, other_shard(d)), device_id_type=MESH,
            )

        for d in (2, 1, 3):
            along_copy(d).start()
        total = bwd_term[x].astype(f32)
        for d in (1, 3, 2):
            scatter_copy(bwd_term, bwd_got, 3, d).wait_recv()
            total = total + bwd_got[lax.rem(x + SHARDS - d, SHARDS)].astype(f32)
        for d in (1, 3, 2):
            along_copy(d).wait_recv()
            row = row + along_got[lax.rem(x + SHARDS - d, SHARDS)][:1, :]
        along = jnp.sum(jnp.where(diagonal, row, 0.0), axis=1, keepdims=True) * (1.0 / WIDTH)
        exact = fwd_all[x].astype(f32) * inverse
        result = up_own[...] + inverse * (total - exact * along)
        bwd_send[...] = pack_rows(result.reshape(REPLICAS, GROUP, FEATURES))
        for t in range(REPLICAS - 1, -1, -1):
            route_copy(bwd_send, peer(t), bwd_recv, 1, t, s - 1).start()
        for d in (1, 3, 2):
            scatter_copy(bwd_term, bwd_got, 3, d).wait_send()
            along_copy(d).wait_send()

    outer_b()
    outer_a()


    def outer_step(w, m, grad, factor, table, q_recv, v_recv):
        def body(k):
            partner = partners[s, table, k, r]
            weight = w[k].astype(f32)
            moment = m[k].astype(f32)
            own = momentum_decay * moment + factor * grad[k]
            new_moment = 0.5 * (own + v_recv[partner].astype(f32))
            kept = 0.5 * (weight + mix_rate * moment + q_recv[partner].astype(f32))
            w[k] = (kept - step_size * new_moment).astype(bf16)
            m[k] = new_moment.astype(bf16)

        each(REPLICAS, body)

    bulk_wait_recv(qb_recv, 0)
    bulk_wait_recv(vb_recv, 2)
    outer_step(wb, mb, grad_b, inner_rate * scale_out, 1, qb_recv, vb_recv)
    stores = [
        pltpu.make_async_copy(src, dst, store_sem.at[i])
        for i, (src, dst) in enumerate([(wb, nwb_h), (mb, nmb_h), (wa, nwa_h), (ma, nma_h)])
    ]
    stores[0].start()
    stores[1].start()
    bulk_wait_recv(qa_recv, 1)
    bulk_wait_recv(va_recv, 3)
    outer_step(wa, ma, grad_a, inner_rate * scale_in, 0, qa_recv, va_recv)
    stores[2].start()
    stores[3].start()

    for d in (1, 2, 3):
        gather_copy(fwd_all, 0, d).wait_send()
        scatter_copy(fwd_term, fwd_got, 1, d).wait_send()
        gather_copy(bwd_all, 2, d).wait_send()

    @pl.when(s < SECTIONS - 1)
    def _():
        route_wait_send(fwd_send, 0)

    @pl.when(s > 0)
    def _():
        route_wait_send(bwd_send, 1)

    for which, src in enumerate((qb_send, qa_send, vb_send, va_send)):
        bulk_wait_send(src, which)
    for copy in stores:
        copy.wait()


def per_device(inputs, targets, weight_a, weight_b, moment_a, moment_b, routes, partners):
    def vmem(*shape, dtype=bf16):
        return pltpu.VMEM(shape, dtype)

    shards = (SHARDS, ROWS, FEATURES)
    routed = (REPLICAS, 2 * GROUP, 128)
    bulk_a = (REPLICAS, PIECE_A, HIDDEN)
    bulk_b = (REPLICAS, PIECE_B, WIDTH)
    dma = pltpu.SemaphoreType.DMA
    shape_a = jax.ShapeDtypeStruct(bulk_a, bf16)
    shape_b = jax.ShapeDtypeStruct(bulk_b, bf16)
    anywhere = pl.BlockSpec(memory_space=pl.ANY)
    smem = pl.BlockSpec(memory_space=pltpu.SMEM)
    new_wa, new_wb, new_ma, new_mb = pl.pallas_call(
        kernel,
        out_shape=(shape_a, shape_b, shape_a, shape_b),
        in_specs=[anywhere] * 6 + [smem, smem],
        out_specs=(anywhere,) * 4,
        scratch_shapes=[
            vmem(ROWS, FEATURES), vmem(ROWS, FEATURES),
            vmem(*bulk_a), vmem(*bulk_b), vmem(*bulk_a), vmem(*bulk_b),
            vmem(*shards), vmem(*shards), vmem(*shards), vmem(REPLICAS, GROUP, FEATURES, dtype=f32),
            vmem(*routed), vmem(*routed),
            vmem(*shards), vmem(*shards), vmem(*shards), vmem(*routed), vmem(*routed),
            vmem(8, ROWS, dtype=f32), vmem(SHARDS, 8, ROWS, dtype=f32),
            vmem(ROWS, FEATURES, dtype=f32),
            vmem(ROWS, 128, dtype=f32), vmem(ROWS, HIDDEN, dtype=f32),
            vmem(HIDDEN, ROWS), vmem(WIDTH, ROWS), vmem(ROWS, HIDDEN),
            vmem(*bulk_a, dtype=f32), vmem(*bulk_b, dtype=f32),
            vmem(*bulk_a), vmem(*bulk_b), vmem(*bulk_a), vmem(*bulk_b),
            vmem(*bulk_a), vmem(*bulk_b), vmem(*bulk_a), vmem(*bulk_b),
            pltpu.SMEM((REPLICAS,), jnp.int32), pltpu.SMEM((REPLICAS,), jnp.int32),
            pltpu.SMEM((REPLICAS,), jnp.int32),
            dma((6,)), dma((4,)), dma((5, SHARDS)), dma((5, SHARDS)), dma((2,)), dma((2,)),
            dma((4,)), dma((4,)),
        ],
        compiler_params=pltpu.CompilerParams(
            collective_id=0, has_side_effects=True, vmem_limit_bytes=56 * 2**20
        ),
    )(
        inputs[0, 0], targets[0, 0], weight_a.reshape(bulk_a), weight_b.reshape(bulk_b),
        moment_a.reshape(bulk_a), moment_b.reshape(bulk_b), routes[0], partners,
    )
    return (
        new_wa.reshape(weight_a.shape), new_wb.reshape(weight_b.shape),
        new_ma.reshape(moment_a.shape), new_mb.reshape(moment_b.shape),
    )


def solution(mesh):
    placed = (
        P("replica", None, None, "shard"),
        P("replica", None, None, "shard"),
        P("replica", "section", None, "shard"),
        P("replica", "section", "shard", None),
        P("replica", "section", None, "shard"),
        P("replica", "section", "shard", None),
        P(),
        P(),
    )
    return jax.shard_map(
        per_device,
        mesh=mesh,
        in_specs=placed,
        out_specs=(
            P("replica", "section", None, "shard"),
            P("replica", "section", "shard", None),
            P("replica", "section", None, "shard"),
            P("replica", "section", "shard", None),
        ),
        check_vma=False,
    )
```

time: 752 us -> 195 us (0.26)
  blocking collectives: 342 us -> 0 us
  waiting for transfers between devices: 208 us -> 0 us
  Pallas kernels: 0 us -> 185 us
  other arithmetic: 52.7 us -> 0 us
  matrix products: 45.5 us -> 0 us
  starting transfers between devices: 44.1 us -> 0 us
  local copies, waits for them, and re-layouts: 42.6 us -> 7.87 us
  between operations: 14.8 us -> 0.65 us
    all_to_all x7 -> x0, blocking collectives: 216 us -> none  [the longest x3 47.5 us: per_device(): lax.all_to_all(send_grouped, 'replica', split_axis=0, concat_axis=0, tile...]
    pallas_call x0 -> x1, Pallas kernels: none -> 185 us  [per_device(): pl.pallas_call(kernel, out_shape=(shape_a, shape_b, shape_a, shape_b), in...]
    reduce_scatter x7 -> x0, waiting for transfers between devices: 151 us -> none  [per_device(): lax.psum_scatter(term.astype(jnp.bfloat16), 'shard', scatter_dimension=1,...]
    all_gather x8 -> x0, blocking collectives: 98.8 us -> none  [the longest x4 49.5 us: per_device(): gathered_up = lax.all_gather(upstream, 'shard', axis=1, tiled=True)]
    all_to_all x5 -> x0, waiting for transfers between devices: 53.7 us -> none  [the longest x1 22.5 us: per_device(): lax.all_to_all(delta_in, 'replica', split_axis=0, concat_axis=0, tiled=True)]
    dot_general x22 -> x0, matrix products: 45.5 us -> none  [the longest x4 15.7 us: per_device(): lax.dot_general(hidden, gathered_up, contract_rows, preferred_element_typ...]
    all_to_all x5 -> x0, starting transfers between devices: 35.9 us -> none  [the longest x3 25.2 us: per_device(): lax.all_to_all(grouped, 'replica', split_axis=0, concat_axis=0, tiled=True)]
    gather x16 -> x0, local copies, waits for them, and re-layouts: 34.5 us -> none  [the longest x3 8.18 us: arrange_out(): jnp.take(array.reshape(replicas, local_hidden // replicas, width), order_...]
  transfers between devices with their start and end apart: 18 -> 0, of which waited for: 16 -> 0; matrix products, arithmetic and copies ran while one was open for 8% -> 0% of each run, Pallas kernels for 0% -> 0%
where the time goes in v1:
time: 195 us; the launch traced here: 193 us
  Pallas kernels  185 us (95%)
  local copies, waits for them, and re-layouts  7.87 us (4%)
    pallas_call x1, Pallas kernels, per_device(): pl.pallas_call(kernel, out_shape=(shape_a, shape_b, shape_a, shape_b), in...  185 us
    unnamed x10, local copies, waits for them, and re-layouts  7.87 us

profile of v1, /device:TPU:32, one launch (start us, length us, event | category | flops | bytes accessed | tf_op | source)
XLA Modules:
  0.0 193.5 jit_solution(15213774341983330875)
XLA Ops:
  0.6 185.0 %shard_map.111 = (bf16[16,64,768]{2,1,0:T(8,128)(2,1)}, bf16[16,48,1024]{2,1,0:T(8,128)(2,1)}, bf16[16,64,768]{2,1,0:T(8,128)(2,1)}, bf16[16,48,1024]{2,1,0:T(8,128)(2,1)}) custom-call(bf16[128,256]{1,0:T(8,128)(2,1)} %bitcast.19, bf16[128,256]{1,0:T(8,128)(2,1)} %bitcast.20, bf16[16,64,768]{2,1,0:T(8,128)(2,1)} %bitcast.15, bf16[16,48,1024]{2,1,0:T(8,128)(2,1)} %bitcast.16, ...), custom_call_target="tpu_custom_call" | custom-call | tf_op jit(solution)/shard_map/pallas_call | solution.py:455
  185.6 0.0 copy-start.2
  185.6 2.8 %copy.16 = bf16[1,1,1024,768]{3,2,1,0:T(8,128)(2,1)} copy(bf16[1,1,1024,768]{3,2,1,0:T(8,128)(2,1)} %bitcast.14) | data formatting | bytes 3145728
  188.4 0.0 copy-done.2
  188.4 0.0 copy-start.1
  188.4 1.1 copy.17
  189.5 0.8 copy-done.1
  190.4 0.0 copy-start
  190.4 1.1 copy.18
  191.5 0.8 copy-done
  192.3 1.1 copy.19
Async XLA Ops:
  185.6 2.8 %copy-start.2 = (bf16[16,48,1024]{2,1,0:T(8,128)(2,1)S(1)}, bf16[16,48,1024]{2,1,0:T(8,128)(2,1)}, u32[]{:S(2)}) copy-start(bf16[16,48,1024]{2,1,0:T(8,128)(2,1)} %get-tuple-element.9) | copy-start | bytes 4718596
  188.4 2.0 %copy-start.1 = (bf16[16,64,768]{2,1,0:T(8,128)(2,1)S(1)}, bf16[16,64,768]{2,1,0:T(8,128)(2,1)}, u32[]{:S(2)}) copy-start(bf16[16,64,768]{2,1,0:T(8,128)(2,1)} %get-tuple-element.10) | copy-start | bytes 4718596
  190.4 2.0 %copy-start = (bf16[16,48,1024]{2,1,0:T(8,128)(2,1)S(1)}, bf16[16,48,1024]{2,1,0:T(8,128)(2,1)}, u32[]{:S(2)}) copy-start(bf16[16,48,1024]{2,1,0:T(8,128)(2,1)} %get-tuple-element.11) | copy-start | bytes 4718596

commit v2 on v1

--- a/solution.py
+++ b/solution.py
@@ -33,6 +33,9 @@
 scale_in = 1.0 / math.sqrt(WIDTH)
 scale_out = 1.0 / math.sqrt(HIDDEN * SHARDS)
 
+RELAYED_B = (15, 14)
+RELAYED_A = (15,)
+
 NN = (((1,), (0,)), ((), ()))
 NT = (((1,), (1,)), ((), ()))
 
@@ -59,19 +62,21 @@
 
 def kernel(
     inp_h, tgt_h, wa_h, wb_h, ma_h, mb_h, routes, partners,
-    nwa_h, nwb_h, nma_h, nmb_h,
+    new_wa, new_wb, new_ma, new_mb,
     inp, tgt, wa, wb, ma, mb,
     fwd_all, fwd_term, fwd_got, fwd_out, fwd_send, fwd_recv,
     bwd_all, bwd_term, bwd_got, bwd_send, bwd_recv, along_send, along_got, up_own,
     inv_rms, slope, hidden_t, normed_t, grad_pre, grad_a, grad_b,
     qa_send, qb_send, qa_recv, qb_recv, va_send, vb_send, va_recv, vb_recv,
     order_f, order_a, order_b,
-    load_sem, store_sem, x_send, x_recv, z_send, z_recv, bulk_send, bulk_recv,
+    load_sem, x_send, x_recv, z_send, z_recv, bulk_send, bulk_recv,
+    relay_b, relay_a, relay_send, relay_recv,
 ):
     r = lax.axis_index("replica")
     s = lax.axis_index("section")
     x = lax.axis_index("shard")
     y, z = r // 8, lax.rem(r, 8)
+    across = (1 - y) * 8 + z
     first, last = s == 0, s == SECTIONS - 1
 
     def other_shard(d):
@@ -117,8 +122,17 @@
 
     each(REPLICAS, lambda t: greet((peer(t), s, x)), 1)
 
+    @pl.when(s >= 2)
+    def _():
+        greet((across, s - 2, x))
+
+    @pl.when(s < 2)
+    def _():
+        greet((lax.rem(z + 4, 8), s + 2, x))
+        greet((8 + lax.rem(z + 4, 8), s + 2, x))
+
     links = jnp.minimum(s, 1) + jnp.minimum(SECTIONS - 1 - s, 1)
-    pl.semaphore_wait(barrier, SHARDS - 1 + REPLICAS - 1 + REPLICAS * links)
+    pl.semaphore_wait(barrier, SHARDS - 1 + REPLICAS - 1 + REPLICAS * links + 1 + s // 2)
 
 
     def gather_copy(ref, phase, d):
@@ -145,7 +159,7 @@
     def route_wait_send(src, phase):
         pltpu.make_async_copy(src, src, z_send.at[phase]).wait()
 
-    def bulk_start(src, dst, which):
+    def bulk_start(src, dst, which, count=REPLICAS):
         def body(t):
             p = peer(t)
             pltpu.make_async_remote_copy(
@@ -153,7 +167,27 @@
                 device_id=(p, s, x), device_id_type=MESH,
             ).start()
 
-        each(REPLICAS, body, 1)
+        each(count, body, 1)
+
+    def late_start(src, dst, which, buffer, relayed):
+        @pl.when(s < 2)
+        def _():
+            for i, t in enumerate(relayed):
+                pltpu.make_async_remote_copy(
+                    src.at[peer(t)], buffer.at[i], bulk_send.at[which], relay_recv.at[which - 2],
+                    device_id=(across, s + 2, x), device_id_type=MESH,
+                ).start()
+
+        bulk_start(src, dst, which, REPLICAS - len(relayed) * jnp.maximum(1 - s // 2, 0))
+
+    def relay(dst, which, buffer, relayed):
+        pltpu.make_async_copy(buffer, buffer, relay_recv.at[which - 2]).wait()
+        for i, t in enumerate(relayed):
+            pltpu.make_async_remote_copy(
+                buffer.at[i], dst.at[across], relay_send.at[which - 2], bulk_recv.at[which],
+                device_id=(lax.rem(1 - y + t % 2, 2) * 8 + lax.rem(z + 4, 8), s - 2, x),
+                device_id_type=MESH,
+            ).start()
 
     def bulk_wait_recv(dst, which):
         part = dst.at[0 : REPLICAS - 1]
@@ -335,7 +369,7 @@
             value = dot(hidden_t[...], bwd_all[j]).reshape(REPLICAS, PIECE_B, FEATURES)
             grad_b[:, :, j * FEATURES : (j + 1) * FEATURES] = value
         fill_v(mb, grad_b, inner_rate * scale_out, order_b, vb_send, vb_recv)
-        bulk_start(vb_send, vb_recv, 2)
+        late_start(vb_send, vb_recv, 2, relay_b, RELAYED_B)
 
     def outer_a():
         for j in range(SHARDS):
@@ -343,7 +377,11 @@
             span = FEATURES // PIECE_A
             grad_a[j * span : (j + 1) * span] = value.reshape(span, PIECE_A, HIDDEN)
         fill_v(ma, grad_a, inner_rate * scale_in, order_a, va_send, va_recv)
-        bulk_start(va_send, va_recv, 3)
+        late_start(va_send, va_recv, 3, relay_a, RELAYED_A)
+
+    @pl.when(s <= 1)
+    def _():
+        outer_b()
 
     @pl.when(s > 0)
     def _():
@@ -388,11 +426,19 @@
             scatter_copy(bwd_term, bwd_got, 3, d).wait_send()
             along_copy(d).wait_send()
 
-    outer_b()
+    @pl.when(s > 1)
+    def _():
+        outer_b()
+
     outer_a()
 
-
-    def outer_step(w, m, grad, factor, table, q_recv, v_recv):
+    @pl.when(s >= 2)
+    def _():
+        relay(vb_recv, 2, relay_b, RELAYED_B)
+        relay(va_recv, 3, relay_a, RELAYED_A)
+
+
+    def outer_step(w, m, grad, factor, table, q_recv, v_recv, new_w, new_m):
         def body(k):
             partner = partners[s, table, k, r]
             weight = w[k].astype(f32)
@@ -400,25 +446,17 @@
             own = momentum_decay * moment + factor * grad[k]
             new_moment = 0.5 * (own + v_recv[partner].astype(f32))
             kept = 0.5 * (weight + mix_rate * moment + q_recv[partner].astype(f32))
-            w[k] = (kept - step_size * new_moment).astype(bf16)
-            m[k] = new_moment.astype(bf16)
+            new_w[k] = (kept - step_size * new_moment).astype(bf16)
+            new_m[k] = new_moment.astype(bf16)
 
         each(REPLICAS, body)
 
     bulk_wait_recv(qb_recv, 0)
     bulk_wait_recv(vb_recv, 2)
-    outer_step(wb, mb, grad_b, inner_rate * scale_out, 1, qb_recv, vb_recv)
-    stores = [
-        pltpu.make_async_copy(src, dst, store_sem.at[i])
-        for i, (src, dst) in enumerate([(wb, nwb_h), (mb, nmb_h), (wa, nwa_h), (ma, nma_h)])
-    ]
-    stores[0].start()
-    stores[1].start()
+    outer_step(wb, mb, grad_b, inner_rate * scale_out, 1, qb_recv, vb_recv, new_wb, new_mb)
     bulk_wait_recv(qa_recv, 1)
     bulk_wait_recv(va_recv, 3)
-    outer_step(wa, ma, grad_a, inner_rate * scale_in, 0, qa_recv, va_recv)
-    stores[2].start()
-    stores[3].start()
+    outer_step(wa, ma, grad_a, inner_rate * scale_in, 0, qa_recv, va_recv, new_wa, new_ma)
 
     for d in (1, 2, 3):
         gather_copy(fwd_all, 0, d).wait_send()
@@ -433,10 +471,13 @@
     def _():
         route_wait_send(bwd_send, 1)
 
+    @pl.when(s >= 2)
+    def _():
+        pltpu.make_async_copy(relay_b, relay_b, relay_send.at[0]).wait()
+        pltpu.make_async_copy(relay_a, relay_a, relay_send.at[1]).wait()
+
     for which, src in enumerate((qb_send, qa_send, vb_send, va_send)):
         bulk_wait_send(src, which)
-    for copy in stores:
-        copy.wait()
 
 
 def per_device(inputs, targets, weight_a, weight_b, moment_a, moment_b, routes, partners):
@@ -448,15 +489,15 @@
     bulk_a = (REPLICAS, PIECE_A, HIDDEN)
     bulk_b = (REPLICAS, PIECE_B, WIDTH)
     dma = pltpu.SemaphoreType.DMA
-    shape_a = jax.ShapeDtypeStruct(bulk_a, bf16)
-    shape_b = jax.ShapeDtypeStruct(bulk_b, bf16)
-    anywhere = pl.BlockSpec(memory_space=pl.ANY)
+    shape_a = pltpu.VMEM(bulk_a, bf16)
+    shape_b = pltpu.VMEM(bulk_b, bf16)
+    far = pl.BlockSpec(memory_space=pltpu.HBM)
     smem = pl.BlockSpec(memory_space=pltpu.SMEM)
     new_wa, new_wb, new_ma, new_mb = pl.pallas_call(
         kernel,
         out_shape=(shape_a, shape_b, shape_a, shape_b),
-        in_specs=[anywhere] * 6 + [smem, smem],
-        out_specs=(anywhere,) * 4,
+        in_specs=[far] * 6 + [smem, smem],
+        out_specs=(pl.BlockSpec(memory_space=pltpu.VMEM),) * 4,
         scratch_shapes=[
             vmem(ROWS, FEATURES), vmem(ROWS, FEATURES),
             vmem(*bulk_a), vmem(*bulk_b), vmem(*bulk_a), vmem(*bulk_b),
@@ -472,8 +513,10 @@
             vmem(*bulk_a), vmem(*bulk_b), vmem(*bulk_a), vmem(*bulk_b),
             pltpu.SMEM((REPLICAS,), jnp.int32), pltpu.SMEM((REPLICAS,), jnp.int32),
             pltpu.SMEM((REPLICAS,), jnp.int32),
-            dma((6,)), dma((4,)), dma((5, SHARDS)), dma((5, SHARDS)), dma((2,)), dma((2,)),
+            dma((6,)), dma((5, SHARDS)), dma((5, SHARDS)), dma((2,)), dma((2,)),
             dma((4,)), dma((4,)),
+            vmem(len(RELAYED_B), PIECE_B, WIDTH), vmem(len(RELAYED_A), PIECE_A, HIDDEN),
+            dma((2,)), dma((2,)),
         ],
         compiler_params=pltpu.CompilerParams(
             collective_id=0, has_side_effects=True, vmem_limit_bytes=56 * 2**20

time: 195 us -> 175 us (0.90)
  Pallas kernels: 185 us -> 168 us
  local copies, waits for them, and re-layouts: 7.87 us -> 4.57 us
    pallas_call x1, Pallas kernels: 185 us -> 168 us  [per_device(): pl.pallas_call(kernel, out_shape=(shape_a, shape_b, shape_a, shape_b), in...]
    unnamed x10 -> x4, local copies, waits for them, and re-layouts: 7.87 us -> 4.57 us
where the time goes in v2:
time: 175 us; the launch traced here: 173 us
  Pallas kernels  168 us (96%)
  local copies, waits for them, and re-layouts  4.57 us (3%)
    pallas_call x1, Pallas kernels, per_device(): pl.pallas_call(kernel, out_shape=(shape_a, shape_b, shape_a, shape_b), in...  168 us
    unnamed x4, local copies, waits for them, and re-layouts  4.57 us

profile of v2, /device:TPU:32, one launch (start us, length us, event | category | flops | bytes accessed | tf_op | source)
XLA Modules:
  0.0 173.0 jit_solution(2460535587839551557)
XLA Ops:
  0.6 167.8 %shard_map.111 = (bf16[16,64,768]{2,1,0:T(8,128)(2,1)S(1)}, bf16[16,48,1024]{2,1,0:T(8,128)(2,1)S(1)}, bf16[16,64,768]{2,1,0:T(8,128)(2,1)S(1)}, bf16[16,48,1024]{2,1,0:T(8,128)(2,1)S(1)}) custom-call(bf16[128,256]{1,0:T(8,128)(2,1)} %bitcast.19, bf16[128,256]{1,0:T(8,128)(2,1)} %bitcast.20, bf16[16,64,768]{2,1,0:T(8,128)(2,1)} %bitcast.15, ...), custom_call_target="tpu_custom_call" | custom-call | tf_op jit(solution)/shard_map/pallas_call | solution.py:496
  168.4 1.1 copy.16
  169.6 1.1 copy.17
  170.7 1.1 copy.18
  171.9 1.1 copy.19

commit v3 on v2

--- a/solution.py
+++ b/solution.py
@@ -33,8 +33,11 @@
 scale_in = 1.0 / math.sqrt(WIDTH)
 scale_out = 1.0 / math.sqrt(HIDDEN * SHARDS)
 
-RELAYED_B = (15, 14)
-RELAYED_A = (15,)
+EARLY_B = (15,)
+EARLY_A = (15,)
+LATE_B = (15, 14)
+LATE_A = (15,)
+FIRST_Q = 7
 
 NN = (((1,), (0,)), ((), ()))
 NT = (((1,), (1,)), ((), ()))
@@ -70,7 +73,7 @@
     qa_send, qb_send, qa_recv, qb_recv, va_send, vb_send, va_recv, vb_recv,
     order_f, order_a, order_b,
     load_sem, x_send, x_recv, z_send, z_recv, bulk_send, bulk_recv,
-    relay_b, relay_a, relay_send, relay_recv,
+    relay_b, relay_a, relay_send, relay_recv, clear,
 ):
     r = lax.axis_index("replica")
     s = lax.axis_index("section")
@@ -122,80 +125,10 @@
 
     each(REPLICAS, lambda t: greet((peer(t), s, x)), 1)
 
-    @pl.when(s >= 2)
-    def _():
-        greet((across, s - 2, x))
-
-    @pl.when(s < 2)
-    def _():
-        greet((lax.rem(z + 4, 8), s + 2, x))
-        greet((8 + lax.rem(z + 4, 8), s + 2, x))
-
-    links = jnp.minimum(s, 1) + jnp.minimum(SECTIONS - 1 - s, 1)
-    pl.semaphore_wait(barrier, SHARDS - 1 + REPLICAS - 1 + REPLICAS * links + 1 + s // 2)
-
-
-    def gather_copy(ref, phase, d):
-        return pltpu.make_async_remote_copy(
-            ref.at[x], ref.at[x], x_send.at[phase, d], x_recv.at[phase, d],
-            device_id=(r, s, other_shard(d)), device_id_type=MESH,
-        )
-
-    def scatter_copy(src, dst, phase, d):
-        return pltpu.make_async_remote_copy(
-            src.at[other_shard(d)], dst.at[x], x_send.at[phase, d], x_recv.at[phase, d],
-            device_id=(r, s, other_shard(d)), device_id_type=MESH,
-        )
-
-    def route_copy(src, slot, dst, phase, t, section):
-        return pltpu.make_async_remote_copy(
-            src.at[slot], dst.at[r], z_send.at[phase], z_recv.at[phase],
-            device_id=(peer(t), section, x), device_id_type=MESH,
-        )
-
-    def route_wait_recv(dst, phase):
-        pltpu.make_async_copy(dst, dst, z_recv.at[phase]).wait()
-
-    def route_wait_send(src, phase):
-        pltpu.make_async_copy(src, src, z_send.at[phase]).wait()
-
-    def bulk_start(src, dst, which, count=REPLICAS):
-        def body(t):
-            p = peer(t)
-            pltpu.make_async_remote_copy(
-                src.at[p], dst.at[r], bulk_send.at[which], bulk_recv.at[which],
-                device_id=(p, s, x), device_id_type=MESH,
-            ).start()
-
-        each(count, body, 1)
-
-    def late_start(src, dst, which, buffer, relayed):
-        @pl.when(s < 2)
-        def _():
-            for i, t in enumerate(relayed):
-                pltpu.make_async_remote_copy(
-                    src.at[peer(t)], buffer.at[i], bulk_send.at[which], relay_recv.at[which - 2],
-                    device_id=(across, s + 2, x), device_id_type=MESH,
-                ).start()
-
-        bulk_start(src, dst, which, REPLICAS - len(relayed) * jnp.maximum(1 - s // 2, 0))
-
-    def relay(dst, which, buffer, relayed):
-        pltpu.make_async_copy(buffer, buffer, relay_recv.at[which - 2]).wait()
-        for i, t in enumerate(relayed):
-            pltpu.make_async_remote_copy(
-                buffer.at[i], dst.at[across], relay_send.at[which - 2], bulk_recv.at[which],
-                device_id=(lax.rem(1 - y + t % 2, 2) * 8 + lax.rem(z + 4, 8), s - 2, x),
-                device_id_type=MESH,
-            ).start()
-
-    def bulk_wait_recv(dst, which):
-        part = dst.at[0 : REPLICAS - 1]
-        pltpu.make_async_copy(part, part, bulk_recv.at[which]).wait()
-
-    def bulk_wait_send(src, which):
-        part = src.at[0 : REPLICAS - 1]
-        pltpu.make_async_copy(part, part, bulk_send.at[which]).wait()
+    other = lax.rem(s + 2, SECTIONS)
+    greet((across, other, x))
+    greet((lax.rem(z + 4, 8), other, x))
+    greet((8 + lax.rem(z + 4, 8), other, x))
 
 
     def invert(table, out):
@@ -220,22 +153,103 @@
         each(REPLICAS, body)
         recv[r] = send[r]
 
-    def fill_v(m, grad, factor, order, send, recv):
+    def make_v(m, grad, factor, order, send):
         def body(p):
             k = order[p]
             value = momentum_decay * m[k].astype(f32) + factor * grad[k]
             send[p] = value.astype(bf16)
 
-        each(REPLICAS, body)
-        recv[r] = send[r]
-
-    def prepare_q():
+        return body
+
+    def prepare_q(needed):
         invert(lambda g: partners[s, 0, g, r], order_a)
         invert(lambda g: partners[s, 1, g, r], order_b)
-        loads[3].wait()
-        loads[4].wait()
+        for i in needed:
+            loads[i].wait()
         fill_q(wb, mb, order_b, qb_send, qb_recv)
         fill_q(wa, ma, order_a, qa_send, qa_recv)
+
+    @pl.when(s > 0)
+    def _():
+        prepare_q((2, 4, 1, 3))
+
+    links = jnp.minimum(s, 1) + jnp.minimum(SECTIONS - 1 - s, 1)
+    pl.semaphore_wait(barrier, SHARDS - 1 + REPLICAS - 1 + REPLICAS * links + 3)
+
+
+    def gather_copy(ref, phase, d):
+        return pltpu.make_async_remote_copy(
+            ref.at[x], ref.at[x], x_send.at[phase, d], x_recv.at[phase, d],
+            device_id=(r, s, other_shard(d)), device_id_type=MESH,
+        )
+
+    def scatter_copy(src, dst, phase, d):
+        return pltpu.make_async_remote_copy(
+            src.at[other_shard(d)], dst.at[x], x_send.at[phase, d], x_recv.at[phase, d],
+            device_id=(r, s, other_shard(d)), device_id_type=MESH,
+        )
+
+    def route_copy(src, slot, dst, phase, t, section):
+        return pltpu.make_async_remote_copy(
+            src.at[slot], dst.at[r], z_send.at[phase], z_recv.at[phase],
+            device_id=(peer(t), section, x), device_id_type=MESH,
+        )
+
+    def route_wait_recv(dst, phase):
+        pltpu.make_async_copy(dst, dst, z_recv.at[phase]).wait()
+
+    def route_wait_send(src, phase):
+        pltpu.make_async_copy(src, src, z_send.at[phase]).wait()
+
+    def bulk_start(src, dst, which, count=REPLICAS, make=None, skip=0, stop=None):
+        def body(t):
+            p = peer(t)
+            if make is not None:
+                make(p)
+            pltpu.make_async_remote_copy(
+                src.at[p], dst.at[r], bulk_send.at[which], bulk_recv.at[which],
+                device_id=(p, s, x), device_id_type=MESH,
+            ).start()
+
+        each(count - 1 if stop is None else stop, lambda i: body(count - 1 - i), skip)
+
+    def detour_start(src, which, buffer, relayed, section, make=None):
+        for i, t in enumerate(relayed):
+            if make is not None:
+                make(peer(t))
+            pltpu.make_async_remote_copy(
+                src.at[peer(t)], buffer.at[i], bulk_send.at[which], relay_recv.at[which],
+                device_id=(across, section, x), device_id_type=MESH,
+            ).start()
+
+    def relay(dst, which, buffer, relayed, section):
+        if not relayed:
+            return
+        part = buffer.at[0 : len(relayed)]
+        pltpu.make_async_copy(part, part, relay_recv.at[which]).wait()
+        for i, t in enumerate(relayed):
+            pltpu.make_async_remote_copy(
+                buffer.at[i], dst.at[across], relay_send.at[which], bulk_recv.at[which],
+                device_id=(lax.rem(1 - y + t % 2, 2) * 8 + lax.rem(z + 4, 8), section, x),
+                device_id_type=MESH,
+            ).start()
+
+    def relay_wait_send(which, buffer, relayed):
+        if not relayed:
+            return
+        part = buffer.at[0 : len(relayed)]
+        pltpu.make_async_copy(part, part, relay_send.at[which]).wait()
+
+    def direct(relayed, upper):
+        return REPLICAS - len(relayed) * (s // 2 if upper else 1 - s // 2)
+
+    def bulk_wait_recv(dst, which):
+        part = dst.at[0 : REPLICAS - 1]
+        pltpu.make_async_copy(part, part, bulk_recv.at[which]).wait()
+
+    def bulk_wait_send(src, which):
+        part = src.at[0 : REPLICAS - 1]
+        pltpu.make_async_copy(part, part, bulk_send.at[which]).wait()
 
     def rows_a(j):
         span = FEATURES // PIECE_A
@@ -254,17 +268,21 @@
 
     @pl.when(s > 0)
     def _():
-        loads[1].wait()
-        loads[2].wait()
-        prepare_q()
+        loads[5].wait()
 
     @pl.when(s >= 2)
     def _():
-        bulk_start(qb_send, qb_recv, 0)
+        detour_start(qb_send, 0, relay_b, EARLY_B, s - 2)
+        detour_start(qa_send, 1, relay_a, EARLY_A, s - 2)
+        bulk_start(qb_send, qb_recv, 0, direct(EARLY_B, True))
 
     @pl.when(last)
     def _():
-        bulk_start(qa_send, qa_recv, 1)
+        bulk_start(qa_send, qa_recv, 1, direct(EARLY_A, True))
+
+    def relay_q():
+        relay(qb_recv, 0, relay_b, EARLY_B, s + 2)
+        relay(qa_recv, 1, relay_a, EARLY_A, s + 2)
 
     @pl.when(s > 0)
     def _():
@@ -280,6 +298,7 @@
         invert(lambda g: routes[link, r, g], order_f)
         loads[1].wait()
         loads[2].wait()
+        loads[5].wait()
 
     preact = jnp.zeros((ROWS, HIDDEN), f32)
     square = jnp.zeros((ROWS, 1), f32)
@@ -296,12 +315,12 @@
     preact = preact * (inverse * scale_in)
     gate = 1.0 / (1.0 + jnp.exp(-preact))
     hidden = (preact * gate).astype(bf16)
-    slope[...] = (gate * (1.0 + preact * (1.0 - gate))) * scale_out
     for d in (2, 1, 3, 0):
         j = other_shard(d)
         fwd_term[j] = (dot(hidden, columns_b(j)) * scale_out).astype(bf16)
         if d:
             scatter_copy(fwd_term, fwd_got, 1, d).start()
+    slope[...] = (gate * (1.0 + preact * (1.0 - gate))) * scale_out
     total = fwd_term[x].astype(f32)
     for d in (1, 3, 2):
         scatter_copy(fwd_term, fwd_got, 1, d).wait_recv()
@@ -318,7 +337,6 @@
 
     @pl.when(last)
     def _():
-        loads[5].wait()
         up = (output - tgt[...].astype(f32)).astype(bf16)
         bwd_all[x] = up
         up_own[...] = up.astype(f32)
@@ -328,17 +346,23 @@
 
     @pl.when(first)
     def _():
-        prepare_q()
+        prepare_q((3, 4))
+        bulk_start(qb_send, qb_recv, 0, stop=FIRST_Q)
+        pl.semaphore_wait(clear, 1)
+        bulk_start(qb_send, qb_recv, 0, skip=FIRST_Q)
+
+    @pl.when(s == 1)
+    def _():
+        pl.semaphore_signal(clear, inc=1, device_id=(r, 0, x), device_id_type=MESH)
         bulk_start(qb_send, qb_recv, 0)
 
-    @pl.when(s == 1)
-    def _():
-        bulk_start(qb_send, qb_recv, 0)
-
     @pl.when(s < SECTIONS - 1)
     def _():
-        loads[5].wait()
-        bulk_start(qa_send, qa_recv, 1)
+        bulk_start(qa_send, qa_recv, 1, direct(EARLY_A, True))
+
+    @pl.when(s < 2)
+    def _():
+        relay_q()
 
     hidden_t[...] = hidden.T
     for j in range(SHARDS):
@@ -368,16 +392,29 @@
         for j in range(SHARDS):
             value = dot(hidden_t[...], bwd_all[j]).reshape(REPLICAS, PIECE_B, FEATURES)
             grad_b[:, :, j * FEATURES : (j + 1) * FEATURES] = value
-        fill_v(mb, grad_b, inner_rate * scale_out, order_b, vb_send, vb_recv)
-        late_start(vb_send, vb_recv, 2, relay_b, RELAYED_B)
+        make = make_v(mb, grad_b, inner_rate * scale_out, order_b, vb_send)
+        @pl.when(s < 2)
+        def _():
+            detour_start(vb_send, 2, relay_b, LATE_B, s + 2, make)
+
+        bulk_start(vb_send, vb_recv, 2, direct(LATE_B, False), make)
+        make(r)
+        vb_recv[r] = vb_send[r]
 
     def outer_a():
         for j in range(SHARDS):
             value = dot(normed_t[j * FEATURES : (j + 1) * FEATURES, :], grad_pre[...])
             span = FEATURES // PIECE_A
             grad_a[j * span : (j + 1) * span] = value.reshape(span, PIECE_A, HIDDEN)
-        fill_v(ma, grad_a, inner_rate * scale_in, order_a, va_send, va_recv)
-        late_start(va_send, va_recv, 3, relay_a, RELAYED_A)
+        make = make_v(ma, grad_a, inner_rate * scale_in, order_a, va_send)
+
+        @pl.when(s < 2)
+        def _():
+            detour_start(va_send, 3, relay_a, LATE_A, s + 2, make)
+
+        bulk_start(va_send, va_recv, 3, direct(LATE_A, False), make)
+        make(r)
+        va_recv[r] = va_send[r]
 
     @pl.when(s <= 1)
     def _():
@@ -434,8 +471,8 @@
 
     @pl.when(s >= 2)
     def _():
-        relay(vb_recv, 2, relay_b, RELAYED_B)
-        relay(va_recv, 3, relay_a, RELAYED_A)
+        relay(vb_recv, 2, relay_b, LATE_B, s - 2)
+        relay(va_recv, 3, relay_a, LATE_A, s - 2)
 
 
     def outer_step(w, m, grad, factor, table, q_recv, v_recv, new_w, new_m):
@@ -473,8 +510,13 @@
 
     @pl.when(s >= 2)
     def _():
-        pltpu.make_async_copy(relay_b, relay_b, relay_send.at[0]).wait()
-        pltpu.make_async_copy(relay_a, relay_a, relay_send.at[1]).wait()
+        relay_wait_send(2, relay_b, LATE_B)
+        relay_wait_send(3, relay_a, LATE_A)
+
+    @pl.when(s < 2)
+    def _():
+        relay_wait_send(0, relay_b, EARLY_B)
+        relay_wait_send(1, relay_a, EARLY_A)
 
     for which, src in enumerate((qb_send, qa_send, vb_send, va_send)):
         bulk_wait_send(src, which)
@@ -515,8 +557,8 @@
             pltpu.SMEM((REPLICAS,), jnp.int32),
             dma((6,)), dma((5, SHARDS)), dma((5, SHARDS)), dma((2,)), dma((2,)),
             dma((4,)), dma((4,)),
-            vmem(len(RELAYED_B), PIECE_B, WIDTH), vmem(len(RELAYED_A), PIECE_A, HIDDEN),
-            dma((2,)), dma((2,)),
+            vmem(2, PIECE_B, WIDTH), vmem(2, PIECE_A, HIDDEN),
+            dma((4,)), dma((4,)), pltpu.SemaphoreType.REGULAR,
         ],
         compiler_params=pltpu.CompilerParams(
             collective_id=0, has_side_effects=True, vmem_limit_bytes=56 * 2**20

time: 175 us -> 171 us (0.977); the launches traced: 173 us -> 171 us
  Pallas kernels: 168 us -> 166 us
    pallas_call x1, Pallas kernels: 168 us -> 166 us  [per_device(): pl.pallas_call(kernel, out_shape=(shape_a, shape_b, shape_a, shape_b), in...]
where the time goes in v3:
time: 171 us
  Pallas kernels  166 us (97%)
  local copies, waits for them, and re-layouts  4.57 us (3%)
    pallas_call x1, Pallas kernels, per_device(): pl.pallas_call(kernel, out_shape=(shape_a, shape_b, shape_a, shape_b), in...  166 us
    unnamed x4, local copies, waits for them, and re-layouts  4.57 us

profile of v3, /device:TPU:32, one launch (start us, length us, event | category | flops | bytes accessed | tf_op | source)
XLA Modules:
  0.0 171.0 jit_solution(8442654443765312060)
XLA Ops:
  0.6 165.8 %shard_map.111 = (bf16[16,64,768]{2,1,0:T(8,128)(2,1)S(1)}, bf16[16,48,1024]{2,1,0:T(8,128)(2,1)S(1)}, bf16[16,64,768]{2,1,0:T(8,128)(2,1)S(1)}, bf16[16,48,1024]{2,1,0:T(8,128)(2,1)S(1)}) custom-call(bf16[128,256]{1,0:T(8,128)(2,1)} %bitcast.19, bf16[128,256]{1,0:T(8,128)(2,1)} %bitcast.20, bf16[16,64,768]{2,1,0:T(8,128)(2,1)} %bitcast.15, ...), custom_call_target="tpu_custom_call" | custom-call | tf_op jit(solution)/shard_map/pallas_call | solution.py:538
  166.4 1.1 copy.16
  167.5 1.1 copy.17
  168.7 1.1 copy.18
  169.8 1.1 copy.19

commit v4 on v3

--- a/solution.py
+++ b/solution.py
@@ -117,13 +117,13 @@
 
     @pl.when(s < SECTIONS - 1)
     def _():
-        each(REPLICAS, lambda t: greet((peer(t), s + 1, x)))
+        each(REPLICAS, lambda t: greet((peer(REPLICAS - 1 - t), s + 1, x)))
 
     @pl.when(s > 0)
     def _():
-        each(REPLICAS, lambda t: greet((peer(t), s - 1, x)))
-
-    each(REPLICAS, lambda t: greet((peer(t), s, x)), 1)
+        each(REPLICAS, lambda t: greet((peer(REPLICAS - 1 - t), s - 1, x)))
+
+    each(REPLICAS - 1, lambda t: greet((peer(REPLICAS - 1 - t), s, x)))
 
     other = lax.rem(s + 2, SECTIONS)
     greet((across, other, x))

time: 171 us -> 171 us (level)
  no operation moved by 1% of the time
where the time goes in v4:
time: 171 us
  Pallas kernels  166 us (97%)
  local copies, waits for them, and re-layouts  4.57 us (3%)
    pallas_call x1, Pallas kernels, per_device(): pl.pallas_call(kernel, out_shape=(shape_a, shape_b, shape_a, shape_b), in...  166 us
    unnamed x4, local copies, waits for them, and re-layouts  4.57 us

profile of v4, /device:TPU:32, one launch (start us, length us, event | category | flops | bytes accessed | tf_op | source)
XLA Modules:
  0.0 170.9 jit_solution(17326214198778065822)
XLA Ops:
  0.6 165.7 %shard_map.111 = (bf16[16,64,768]{2,1,0:T(8,128)(2,1)S(1)}, bf16[16,48,1024]{2,1,0:T(8,128)(2,1)S(1)}, bf16[16,64,768]{2,1,0:T(8,128)(2,1)S(1)}, bf16[16,48,1024]{2,1,0:T(8,128)(2,1)S(1)}) custom-call(bf16[128,256]{1,0:T(8,128)(2,1)} %bitcast.19, bf16[128,256]{1,0:T(8,128)(2,1)} %bitcast.20, bf16[16,64,768]{2,1,0:T(8,128)(2,1)} %bitcast.15, ...), custom_call_target="tpu_custom_call" | custom-call | tf_op jit(solution)/shard_map/pallas_call | solution.py:538
  166.3 1.1 copy.16
  167.5 1.1 copy.17
  168.6 1.1 copy.18
  169.8 1.1 copy.19
